TPU v7x, 32 devices: a whole 2x2x4 slice. The times are simulated.
32 devices in a mesh: segment: 4 (over y, core), ctx: 4 (over z), tp: 2 (over x).
Axes of the slice: x: 2, y: 2, z: 4, core: 2. Of those that a mesh axis runs over, the one named last changes fastest.
Arguments:
- held: bfloat16 [4, 1024, 3584], P('segment', 'ctx'), may hold values from -6 to 6
- text: bfloat16 [1024, 3584], P('ctx'), may hold values from -6 to 6
- frames: bfloat16 [512, 1024], P('ctx'), may hold values from -6 to 6
- join: int32 [8], P('ctx'), may hold values from 0 to 960, as said below
- ln_gain: float32 [1024], replicated, may hold values from 0.1 to 1.9
- w_proj: bfloat16 [1024, 3584], P('tp'), may hold values from -0.1875 to 0.1875
- b_proj: float32 [3584], replicated, may hold values from -3 to 3
- norm_gain: float32 [3, 3584], replicated, may hold values from 0.1 to 1.9
- w_qkv: bfloat16 [3, 3584, 2304], P(None, 'ctx', 'tp'), may hold values from -0.09375 to 0.09375
- b_qkv: float32 [3, 2304], P(None, 'tp'), may hold values from -4 to 4
- w_out: bfloat16 [3, 1792, 3584], P(None, 'tp', 'ctx'), may hold values from -1.5 to 1.5
Outputs:
- segment_out: bfloat16 [4, 1024, 3584], P('segment', 'ctx')
Inputs may be any that keep to these rules, and one draw needn't show every extreme that they name: `join`: frames never intersect; the 2 frames f with f // 2 == d lie in order inside positions d * 256 to (d + 1) * 256 - 1.
All inputs are finite; a program needn't handle non-finite values.
Results may differ from a plain program's by a relative error of at most 0.015.
Values may be sent and summed in bfloat16 or wider, within the bound.
A program may use at most 128 MiB of HBM per device.

v0:
```python
from functools import partial

import jax
import jax.numpy as jnp
from jax import lax
from jax.sharding import PartitionSpec as P

HD = 128
GROUP = 7
FRAME = 64


def shifted(value, axis, by):
    devices = lax.axis_size(axis)
    pairs = [(i, i + by) for i in range(devices) if 0 <= i + by < devices]
    return lax.ppermute(value, axis, pairs)


def update_state(softmax_state, query_flat, query_pos, keys_in, values_in, offset):
    peak_old, total_old, accum_old = softmax_state
    key_pos = jnp.arange(keys_in.shape[0], dtype=jnp.int32)
    scores = jnp.dot(query_flat, keys_in.T, preferred_element_type=jnp.float32) * HD ** (-0.5)
    allowed = key_pos[None, :] <= query_pos[:, None]
    scores = jnp.where(allowed, scores, -1e30)
    peak_new = jnp.maximum(peak_old, jnp.max(scores, axis=1))
    weights = jnp.where(allowed, jnp.exp(scores - peak_new[:, None]), 0.0)
    total_new = jnp.sum(weights, axis=1)
    accum_new = jnp.dot(weights.astype(jnp.bfloat16), values_in, preferred_element_type=jnp.float32)
    return (peak_new, total_new, accum_new)


def keep_state(softmax_state):
    return softmax_state


def on_device(held, text, frames, join, ln_gain, w_proj, b_proj, norm_gain, w_qkv, b_qkv, w_out):
    segment_id = lax.axis_index("segment")
    ctx_id = lax.axis_index("ctx")
    tp_id = lax.axis_index("tp")
    hidden_in = shifted(held[0], "segment", 1)
    tok_rows = hidden_in.shape[0]
    half_rows = tok_rows // 2
    layer_id = jnp.maximum(segment_id - 1, 0)
    weight_qkv = lax.dynamic_index_in_dim(w_qkv, layer_id, 0, keepdims=False)
    bias_qkv = lax.dynamic_index_in_dim(b_qkv, layer_id, 0, keepdims=False)
    layer_gain = lax.dynamic_index_in_dim(norm_gain, layer_id, 0, keepdims=False)
    weight_out = lax.dynamic_index_in_dim(w_out, layer_id, 0, keepdims=False)
    inputs = hidden_in.astype(jnp.float32)
    normed = (
        inputs * lax.rsqrt(jnp.mean(inputs * inputs, axis=1, keepdims=True) + 1e-06) * layer_gain
    ).astype(jnp.bfloat16)
    merged = jnp.dot(
        normed,
        lax.all_gather(weight_qkv, "ctx", axis=0, tiled=True),
        preferred_element_type=jnp.float32,
    )
    merged = (merged + bias_qkv).astype(jnp.bfloat16)
    query_cols = GROUP * HD
    queries = merged[:, :query_cols]
    key_part = merged[:, query_cols : query_cols + HD]
    value_part = merged[:, query_cols + HD : query_cols + 2 * HD]
    local_steps = jnp.arange(half_rows, dtype=jnp.int32)
    first_pos = ctx_id * tok_rows + local_steps
    second_q = queries[half_rows:]
    second_pos = ctx_id * tok_rows + half_rows + local_steps
    first_flat = queries[:half_rows].reshape(half_rows * GROUP, HD)
    second_flat = second_q.reshape(half_rows * GROUP, HD)
    first_qpos = jnp.repeat(first_pos, GROUP)
    second_qpos = jnp.repeat(second_pos, GROUP)
    flat_rows = half_rows * GROUP
    empty = (
        jnp.full((flat_rows,), -1e30, jnp.float32),
        jnp.zeros((flat_rows,), jnp.float32),
        jnp.zeros((flat_rows, HD), jnp.float32),
    )
    carried = (empty, empty)
    offset = jnp.int32(0)
    keys_in = lax.all_gather(key_part, "ctx", axis=0, tiled=True)
    values_in = lax.all_gather(value_part, "ctx", axis=0, tiled=True)
    updated = []
    for softmax_state, query_flat, query_pos in (
        (carried[0], first_flat, first_qpos),
        (carried[1], second_flat, second_qpos),
    ):
        step_fn = partial(
            update_state,
            query_flat=query_flat,
            query_pos=query_pos,
            keys_in=keys_in,
            values_in=values_in,
            offset=offset,
        )
        updated.append(lax.cond(offset <= jnp.max(query_pos), step_fn, keep_state, softmax_state))

    def finish(softmax_state):
        return (
            (softmax_state[2] / softmax_state[1][:, None])
            .astype(jnp.bfloat16)
            .reshape(half_rows, GROUP * HD)
        )

    first_out = finish(updated[0])
    second_out = finish(updated[1])
    attended = jnp.concatenate([first_out, second_out], axis=0)
    partial_model = jnp.dot(
        attended,
        lax.all_gather(weight_out, "ctx", axis=1, tiled=True),
        preferred_element_type=jnp.float32,
    )
    positions = ctx_id * tok_rows + jnp.arange(tok_rows, dtype=jnp.int32)[:, None]
    starts = join[None, :]
    inside = (positions >= starts) & (positions < starts + FRAME)
    frame_base = (jnp.arange(join.shape[0], dtype=jnp.int32) * FRAME)[None, :]
    source = jnp.sum(jnp.where(inside, frame_base + positions - starts, 0), axis=1)
    is_vision = jnp.any(inside, axis=1)

    def vision_term():
        frame_in = frames.astype(jnp.float32)
        center = jnp.mean(frame_in, axis=1, keepdims=True)
        spread = jnp.mean((frame_in - center) * (frame_in - center), axis=1, keepdims=True)
        normed_frames = ((frame_in - center) * lax.rsqrt(spread + 1e-06) * ln_gain).astype(
            jnp.bfloat16
        )
        vis_width = w_proj.shape[0]
        normed_half = lax.dynamic_slice_in_dim(normed_frames, tp_id * vis_width, vis_width, 1)
        projected = jnp.dot(normed_half, w_proj, preferred_element_type=jnp.float32)
        return jnp.where(is_vision[:, None], jnp.take(projected, source, axis=0), 0.0)

    def model_term():
        return partial_model

    is_first = segment_id == 0
    section_term = lax.cond(is_first, vision_term, model_term)
    baseline = jnp.where(
        is_first, jnp.where(is_vision[:, None], b_proj[None, :], text.astype(jnp.float32)), inputs
    )
    summed = lax.psum(section_term.astype(jnp.bfloat16), "tp").astype(jnp.float32)
    result = (baseline + summed).astype(jnp.bfloat16)
    return result[None]


def solution(mesh):
    return jax.shard_map(
        on_device,
        mesh=mesh,
        in_specs=(
            P("segment", "ctx", None),
            P("ctx", None),
            P("ctx", None),
            P("ctx"),
            P(),
            P("tp", None),
            P(),
            P(),
            P(None, "ctx", "tp"),
            P(None, "tp"),
            P(None, "tp", "ctx"),
        ),
        out_specs=P("segment", "ctx", None),
        check_vma=False,
    )
```

profile of v0, /device:TPU:1, one launch (start us, length us, event | category | flops | bytes accessed | tf_op | source)
XLA Modules:
  0.0 362.6 jit_solution(8803751301710413790)
XLA Ops:
  6.5 0.0 copy-start
  6.5 0.0 all-gather.5.cloned.1.call-start
  6.5 3.1 constant_dynamic-slice_fusion.1
  9.6 0.0 copy-start.4
  9.6 0.0 all-gather.5.cloned.1.call-update
  9.6 0.0 all-gather.7.cloned.1.call-start
  9.7 2.7 constant_dynamic-slice_fusion
  12.4 0.0 all-gather.7.cloned.1.call-update
  12.4 0.0 all-reduce.2.cloned.1.call-start
  12.5 4.5 %collective-permute-start = (bf16[256,3584]{1,0:T(8,128)(2,1)}, bf16[256,3584]{1,0:T(8,128)(2,1)S(1)}, u32[]{:S(2)}, u32[]{:S(2)}) collective-permute-start(bf16[256,3584]{1,0:T(8,128)(2,1)} %bitcast.20), channel_id=1, source_target_pairs={{0,8},{8,16},{16,24},{1,9},{9,17},{17,25},{2,10},{10,18},{18,26},{... | collective-permute-start | bytes 5505032 | tf_op jit(solution)/shard_map/ppermute | solution.py:16
  17.0 0.7 broadcast_reduce_fusion.1
  18.4 0.7 broadcast_reduce_fusion
  19.8 0.0 copy-done.4
  19.9 0.1 fusion.48
  20.0 0.1 ge.21
  20.0 0.7 dynamic-slice_reduce_fusion.1
  20.8 0.0 copy-done
  20.9 16.6 %collective-permute-done = bf16[256,3584]{1,0:T(8,128)(2,1)S(1)} collective-permute-done((bf16[256,3584]{1,0:T(8,128)(2,1)}, bf16[256,3584]{1,0:T(8,128)(2,1)S(1)}, u32[]{:S(2)}, u32[]{:S(2)}) %collective-permute-start) | collective-permute-done | bytes 1835040 | tf_op jit(solution)/shard_map/ppermute | solution.py:16
  37.5 0.0 copy-start.1
  37.5 0.4 fusion.31
  37.9 121.7 %all-gather.5.cloned.1.call-done = bf16[1,3584,1152]{2,1,0:T(8,128)(2,1)} async-done(((bf16[1,896,1152]{2,1,0:T(8,128)(2,1)}), bf16[1,3584,1152]{2,1,0:T(8,128)(2,1)}) %all-gather.5.cloned.1.call-update) | async-done | bytes 8257552 | tf_op jit(solution)/shard_map/all_gather | solution.py:54
  159.6 6.0 %fusion.37 = bf16[256,1152]{1,0:T(8,128)(2,1)S(1)} fusion(bf16[1,3584,1152]{2,1,0:T(8,128)(2,1)} %all-gather.5.cloned.1.call-done, bf16[256,3584]{1,0:T(8,128)(2,1)S(1)} %collective-permute-done, f32[3584]{0:T(1024)S(1)} %dynamic-slice_reduce_fusion, f32[256]{0:T(256)S(1)} %add_rsqrt_fusion.1, f32[1152]{0:T(1024)S(1)} %dynamic-slice_reduce_fusion.1), kind=kOutput, calls=%fused_computation.56 | convolution fusion | flops 2118189056 | bytes 10702336 | tf_op jit(solution)/shard_map/dot_general | solution.py:52
  165.6 0.0 copy-done.1
  165.6 12.9 %all_gather.13 = bf16[1024,128]{1,0:T(8,128)(2,1)S(1)} all-gather(bf16[256,128]{1,0:T(8,128)(2,1)S(1)} %get-tuple-element.92), channel_id=1, replica_groups=mesh['segment'=4,'ctx'=4,'tp'=2] {'ctx'}, dimensions={0}, use_global_device_ids=true | all-gather | bytes 327680 | tf_op jit(solution)/shard_map/all_gather | solution.py:78
  178.4 20.3 %all_gather.14 = bf16[1024,128]{1,0:T(8,128)(2,1)S(1)} all-gather(bf16[256,128]{1,0:T(8,128)(2,1)S(1)} %get-tuple-element.91), channel_id=1, replica_groups=mesh['segment'=4,'ctx'=4,'tp'=2] {'ctx'}, dimensions={0}, use_global_device_ids=true | all-gather | bytes 327680 | tf_op jit(solution)/shard_map/all_gather | solution.py:79
  198.8 0.1 broadcast_in_dim.104
  198.8 4.1 %conditional.3 = (f32[896]{0:T(1024)S(1)}, f32[896,128]{1,0:T(8,128)S(1)}) conditional(s32[]{:T(128)} %convert_element_type.51, () %tuple.27, (s32[128,7]{1,0:T(8,128)S(1)}, bf16[256,1152]{1,0:T(8,128)(2,1)S(1)}, bf16[1024,128]{1,0:T(8,128)(2,1)S(1)}, bf16[1024,128]{1,0:T(8,128)(2,1)S(1)}) %tuple.28), branch_computations={%region_3.4_spmd, %region_4.7_spmd} | conditional | flops 484441216 | bytes 13179408 | solution.py:93
  198.8 0.2 le.30
  199.1 0.2 reshape.63
  199.3 0.9 fusion
  200.2 1.5 fusion.3
  201.7 1.2 fusion.2
  202.9 0.2 divide_convert_fusion.1
  203.1 0.2 reshape.67
  203.4 0.1 broadcast_in_dim.105
  203.4 0.0 copy-start.2
  203.5 0.0 copy-start.5
  203.5 4.3 %conditional.4 = (f32[896]{0:T(1024)S(1)}, f32[896,128]{1,0:T(8,128)S(1)}) conditional(s32[]{:T(128)} %convert_element_type.55, () %tuple.29, (s32[128,7]{1,0:T(8,128)S(1)}, bf16[256,1152]{1,0:T(8,128)(2,1)S(1)}, bf16[1024,128]{1,0:T(8,128)(2,1)S(1)}, bf16[1024,128]{1,0:T(8,128)(2,1)S(1)}) %tuple.30), branch_computations={%region_8.9_spmd, %region_9.12_spmd} | conditional | flops 484441216 | bytes 13179408 | solution.py:93
  203.5 0.2 le.38
  203.7 0.2 reshape.64
  204.0 0.9 fusion.8
  204.8 1.5 fusion.11
  206.3 1.2 fusion.10
  207.7 0.2 divide_convert_fusion
  207.9 0.2 reshape.68
  208.2 75.1 %all-gather.7.cloned.1.call-done = bf16[1,896,3584]{2,1,0:T(8,128)(2,1)} async-done(((bf16[1,896,896]{2,1,0:T(8,128)(2,1)}), bf16[1,896,3584]{2,1,0:T(8,128)(2,1)}) %all-gather.7.cloned.1.call-update) | async-done | bytes 6422544 | tf_op jit(solution)/shard_map/all_gather | solution.py:107
  283.2 0.0 copy-done.2
  283.2 0.0 copy-done.5
  283.2 6.1 %fusion.27 = bf16[256,3584]{1,0:T(8,128)(2,1)} fusion(bf16[1,896,3584]{2,1,0:T(8,128)(2,1)} %all-gather.7.cloned.1.call-done, bf16[128,896]{1,0:T(8,128)(2,1)S(1)} %reshape.68, bf16[128,896]{1,0:T(8,128)(2,1)S(1)} %reshape.67), kind=kOutput, calls=%fused_computation.45 | convolution fusion | flops 1645084672 | bytes 8716288 | tf_op jit(solution)/shard_map/dot_general | solution.py:105
  289.4 0.0 copy-start.3
  289.4 0.0 all-reduce.2.cloned.1.call-update
  289.4 61.9 %all-reduce.2.cloned.1.call-done = bf16[256,3584]{1,0:T(8,128)(2,1)} async-done(((bf16[256,3584]{1,0:T(8,128)(2,1)}), bf16[256,3584]{1,0:T(8,128)(2,1)}) %all-reduce.2.cloned.1.call-update) | async-done | bytes 1835024 | tf_op jit(solution)/shard_map/psum | solution.py:137
  351.3 0.0 copy-done.3
  351.3 4.8 %fusion.41 = bf16[1,256,3584]{2,1,0:T(8,128)(2,1)} fusion(bf16[256,3584]{1,0:T(8,128)(2,1)} %all-reduce.2.cloned.1.call-done, bf16[256,3584]{1,0:T(8,128)(2,1)} %copy-done.1, bf16[256,3584]{1,0:T(8,128)(2,1)} %param.18, f32[3584]{0:T(1024)S(1)} %copy-done.3, pred[256]{0:T(512)(128)(4,1)S(1)} %get-tuple-element.83, pred[]{:T(512)S(6)} %eq.3), kind=kLoop, calls=%fused_computation.57 | loop fusion | flops 6422528 | bytes 7354625 | tf_op jit(solution)/shard_map/broadcast_in_dim | solution.py:139
  (14 shorter events, 0.1 us)
Async XLA Ops:
  6.5 14.3 %copy-start = (f32[3,3584]{1,0:T(4,128)S(1)}, f32[3,3584]{1,0:T(4,128)}, u32[]{:S(2)}) copy-start(f32[3,3584]{1,0:T(4,128)} %param.24) | copy-start | bytes 129028
  6.5 153.1 %all-gather.5.cloned.1.call-start = ((), (), s32[]{:S(2)}) async-start(), calls=%async_computation.1 | async-start | bytes 10321920 | tf_op jit(solution)/shard_map/all_gather | solution.py:54
  9.6 10.2 %copy-start.4 = (s32[2]{0:T(128)S(1)}, s32[2]{0:T(128)}, u32[]{:S(2)}) copy-start(s32[2]{0:T(128)} %param.20) | copy-start | bytes 28
  9.6 273.6 %all-gather.7.cloned.1.call-start = ((), (), s32[]{:S(2)}) async-start(), calls=%async_computation.2 | async-start | bytes 8028160 | tf_op jit(solution)/shard_map/all_gather | solution.py:107
  12.4 338.8 %all-reduce.2.cloned.1.call-start = ((), (), s32[]{:S(2)}) async-start(), calls=%async_computation | async-start | bytes 3670016 | tf_op jit(solution)/shard_map/psum | solution.py:137
  12.5 25.0 %collective-permute-start = (bf16[256,3584]{1,0:T(8,128)(2,1)}, bf16[256,3584]{1,0:T(8,128)(2,1)S(1)}, u32[]{:S(2)}, u32[]{:S(2)}) collective-permute-start(bf16[256,3584]{1,0:T(8,128)(2,1)} %bitcast.20), channel_id=1, source_target_pairs={{0,8},{8,16},{16,24},{1,9},{9,17},{17,25},{2,10},{10,18},{18,26},{... | collective-permute-start | bytes 5505032 | tf_op jit(solution)/shard_map/ppermute | solution.py:16
  37.5 128.1 %copy-start.1 = (bf16[256,3584]{1,0:T(8,128)(2,1)}, bf16[256,3584]{1,0:T(8,128)(2,1)S(1)}, u32[]{:S(2)}) copy-start(bf16[256,3584]{1,0:T(8,128)(2,1)S(1)} %collective-permute-done) | copy-start | bytes 5505028
  203.4 79.8 %copy-start.2 = (bf16[128,1024]{1,0:T(8,128)(2,1)S(1)}, bf16[128,1024]{1,0:T(8,128)(2,1)}, u32[]{:S(2)}) copy-start(bf16[128,1024]{1,0:T(8,128)(2,1)} %param.19) | copy-start | bytes 786436
  203.5 79.8 %copy-start.5 = (f32[1024]{0:T(1024)S(1)}, f32[1024]{0:T(1024)}, u32[]{:S(2)}) copy-start(f32[1024]{0:T(1024)} %param.21) | copy-start | bytes 12292
  289.4 61.9 %copy-start.3 = (f32[3584]{0:T(1024)S(1)}, f32[3584]{0:T(1024)}, u32[]{:S(2)}) copy-start(f32[3584]{0:T(1024)} %param.23) | copy-start | bytes 43012
Sparse Core Ops, SparseCore 0:
  9.8 149.7 all-gather.4
  161.2 121.9 all-gather.6
  289.5 61.7 all-reduce.1
where the time goes:
time: 364 us; the launch traced here: 363 us
  waiting for transfers between devices  275 us (76%)
  blocking collectives  33.2 us (9%)
  matrix products  16.7 us (5%)
  between operations  14.6 us (4%)
  other arithmetic  9.7 us (3%)
  local copies, waits for them, and re-layouts  8.27 us (2%)
  starting transfers between devices  4.62 us (1%)
    all_gather x1, waiting for transfers between devices, on_device(): lax.all_gather(weight_qkv, 'ctx', axis=0, tiled=True)  122 us
    all_gather x1, waiting for transfers between devices, on_device(): lax.all_gather(weight_out, 'ctx', axis=1, tiled=True)  75.1 us
    psum x1, waiting for transfers between devices, on_device(): lax.psum(section_term.astype(jnp.bfloat16), 'tp').astype(jnp.float32)  61.9 us
    all_gather x1, blocking collectives, on_device(): values_in = lax.all_gather(value_part, 'ctx', axis=0, tiled=True)  20.3 us
    ppermute x1, waiting for transfers between devices, shifted(): return lax.ppermute(value, axis, pairs)  16.6 us
    all_gather x1, blocking collectives, on_device(): keys_in = lax.all_gather(key_part, 'ctx', axis=0, tiled=True)  12.9 us
  transfers between devices with their start and end apart: 4, of which 4 were waited for; matrix products, arithmetic and copies ran while one was open for 6% of the time, Pallas kernels for 0%

commit v1 on v0

--- a/solution.py
+++ b/solution.py
@@ -3,6 +3,8 @@
 import jax
 import jax.numpy as jnp
 from jax import lax
+from jax.experimental import pallas as pl
+from jax.experimental.pallas import tpu as pltpu
 from jax.sharding import PartitionSpec as P
 
 HD = 128
@@ -139,9 +141,406 @@
     return result[None]
 
 
+def relay_kernel(
+    sizes,
+    held, text, frames, join, ln_gain, w_proj, b_proj, norm_gain, w_qkv, b_qkv, w_out,
+    out,
+    held_v, rs_out, rs_in, x_v, wq_v, wo_v, own_sum, part_out, part_in, merged_v, kv_v, att_v,
+    vis_v, wp_v, text_v, half_out, half_in, half_own, res_v,
+    load_sem, store_sem, x_send, x_recv, rs_send, rs_recv, fwd_send, fwd_recv,
+    part_send, part_recv, kv_send, kv_recv, att_send, att_recv,
+    half_send, half_recv, res_send, res_recv, pair_send, pair_recv,
+):
+    segs, n, rows, width = sizes
+    half = rows // 2
+    s = lax.axis_index("segment")
+    c = lax.axis_index("ctx")
+    t = lax.axis_index("tp")
+    layer = jnp.maximum(s - 1, 0)
+    is_layer = s > 0
+    feeds = s < segs - 1
+    query_cols = GROUP * HD
+
+    def remote(src, dst, send, recv, segment, ctx, tp):
+        return pltpu.make_async_remote_copy(
+            src_ref=src, dst_ref=dst, send_sem=send, recv_sem=recv,
+            device_id={"segment": segment, "ctx": ctx, "tp": tp},
+            device_id_type=pl.DeviceIdType.MESH,
+        )
+
+    def cols(k):
+        return pl.ds(pl.multiple_of(k * width, 128), width)
+
+    def turn(d):
+        return lax.rem(c + d, n)
+
+    loads = {
+        "held": pltpu.make_async_copy(held, held_v, load_sem.at[0]),
+        "wq": pltpu.make_async_copy(w_qkv.at[layer], wq_v, load_sem.at[1]),
+        "wo": pltpu.make_async_copy(w_out.at[layer], wo_v, load_sem.at[2]),
+        "wp": pltpu.make_async_copy(w_proj, wp_v, load_sem.at[3]),
+        "text": pltpu.make_async_copy(text, text_v, load_sem.at[4]),
+    }
+
+    @pl.when(feeds)
+    def _():
+        loads["held"].start()
+
+    @pl.when(is_layer)
+    def _():
+        loads["wq"].start()
+        loads["wo"].start()
+
+    @pl.when(s == 0)
+    def _():
+        loads["wp"].start()
+        loads["text"].start()
+
+    barrier = pltpu.get_barrier_semaphore()
+
+    def greet(segment, ctx, tp):
+        pl.semaphore_signal(
+            barrier, inc=1, device_id={"segment": segment, "ctx": ctx, "tp": tp},
+            device_id_type=pl.DeviceIdType.MESH,
+        )
+
+    greet(s, c, 1 - t)
+    for d in range(1, n):
+        greet(s, turn(d), t)
+
+    @pl.when(feeds)
+    def _():
+        for d in range(n):
+            greet(s + 1, turn(d), t)
+
+    @pl.when(is_layer)
+    def _():
+        for d in range(n):
+            greet(s - 1, turn(d), t)
+
+    peers = n + n * jnp.minimum(s, 1) + n * jnp.minimum(segs - 1 - s, 1)
+    pl.semaphore_wait(barrier, peers)
+
+    def x_copy(k):
+        return remote(
+            held.at[pl.ds(pl.multiple_of(t * half, 16), half), cols(k)], x_v.at[c, t],
+            x_send.at[k], x_recv.at[c], s + 1, k, t,
+        )
+
+    def rs_copy():
+        return remote(rs_out, rs_in, rs_send.at[0], rs_recv.at[0], s + 1, c, t)
+
+    def fwd_copy(j, side):
+        return remote(
+            x_v.at[j, side], x_v.at[j, side], fwd_send.at[j], fwd_recv.at[j], s, c, 1 - t
+        )
+
+    def part_copy(j, slot):
+        return remote(
+            part_out.at[j], part_in.at[slot], part_send.at[j], part_recv.at[slot], s, j, t
+        )
+
+    def kv_copy(j, slot):
+        return remote(kv_v.at[slot], kv_v.at[slot], kv_send.at[j], kv_recv.at[slot], s, j, t)
+
+    def att_copy(j, slot):
+        return remote(att_v.at[slot], att_v.at[slot], att_send.at[j], att_recv.at[slot], s, j, t)
+
+    def half_copy(j):
+        return remote(
+            half_out.at[j], half_in.at[j], half_send.at[j], half_recv.at[j], s, c, 1 - t
+        )
+
+    def res_copy(j, slot):
+        return remote(
+            half_out.at[n + j], res_v.at[slot, t], res_send.at[j], res_recv.at[slot], s, j, t
+        )
+
+    def pair_copy(k, side):
+        return remote(
+            res_v.at[k, side], res_v.at[k, side], pair_send.at[k], pair_recv.at[k], s, c, 1 - t
+        )
+
+    def out_copy(k, side):
+        return pltpu.make_async_copy(
+            res_v.at[k, side],
+            out.at[pl.ds(pl.multiple_of(side * half, 16), half), cols(k)],
+            store_sem.at[k, side],
+        )
+
+    @pl.when(feeds)
+    def _():
+        for d in range(n):
+            x_copy(turn(d)).start()
+        loads["held"].wait()
+
+        @pl.loop(0, rows // 32)
+        def _(i):
+            at = pl.ds(pl.multiple_of(i * 32, 32), 32)
+            x = held_v[at, :].astype(jnp.float32)
+            scale = lax.rsqrt(jnp.mean(x * x, axis=1, keepdims=True) + 1e-06)
+            rs_out[at, :] = jnp.broadcast_to(scale, (32, HD))
+
+        rs_copy().start()
+
+    @pl.when(s == 0)
+    def _():
+        frame_in = frames[...].astype(jnp.float32)
+        center = jnp.mean(frame_in, axis=1, keepdims=True)
+        spread = jnp.mean((frame_in - center) * (frame_in - center), axis=1, keepdims=True)
+        normed = ((frame_in - center) * lax.rsqrt(spread + 1e-06) * ln_gain[...]).astype(
+            jnp.bfloat16
+        )
+        vis_width = w_proj.shape[0]
+        normed = jnp.where(t == 0, normed[:, :vis_width], normed[:, vis_width:])
+        count = frames.shape[0]
+        token = lax.broadcasted_iota(jnp.int32, (half, count), 1)
+        for side in range(2):
+            position = c * rows + side * half + lax.broadcasted_iota(jnp.int32, (half, count), 0)
+            pick = jnp.zeros((half, count), jnp.float32)
+            for f in range(count // FRAME):
+                mine = (token >= f * FRAME) & (token < (f + 1) * FRAME)
+                hit = mine & (position - join[f] == token - f * FRAME)
+                pick = jnp.where(hit, 1.0, pick)
+            vis_v[side] = jnp.dot(
+                pick.astype(jnp.bfloat16), normed, preferred_element_type=jnp.float32
+            ).astype(jnp.bfloat16)
+        loads["wp"].wait()
+        loads["text"].wait()
+
+        @pl.loop(0, n)
+        def _(k):
+            half_out[k] = jnp.dot(
+                vis_v[1 - t], wp_v[:, cols(k)], preferred_element_type=jnp.float32
+            ).astype(jnp.bfloat16)
+            half_copy(k).start()
+            half_own[k] = jnp.dot(
+                vis_v[t], wp_v[:, cols(k)], preferred_element_type=jnp.float32
+            )
+
+        place = c * rows + t * half + lax.broadcasted_iota(jnp.int32, (half, width), 0)
+        inside = jnp.zeros((half, width), jnp.bool_)
+        for f in range(count // FRAME):
+            inside = inside | ((place >= join[f]) & (place < join[f] + FRAME))
+
+        @pl.loop(0, n)
+        def _(k):
+            half_copy(k).wait_recv()
+            total = half_own[k] + half_in[k].astype(jnp.float32) + b_proj[:, cols(k)]
+            base = text_v[pl.ds(pl.multiple_of(t * half, 16), half), cols(k)].astype(jnp.float32)
+            res_v[k, t] = jnp.where(inside, total, base).astype(jnp.bfloat16)
+            pair_copy(k, t).start()
+            out_copy(k, t).start()
+
+    @pl.when(is_layer)
+    def _():
+        loads["wq"].wait()
+        gain = norm_gain[pl.ds(layer, 1), cols(c)]
+
+        @pl.loop(0, n)
+        def _(d):
+            j = turn(d)
+            x_wait = remote(
+                x_v.at[j, t], x_v.at[j, t], x_send.at[j], x_recv.at[j], s, c, 1 - t
+            )
+            x_wait.wait_recv()
+            fwd_copy(j, t).start()
+
+        @pl.loop(0, n)
+        def _(d):
+            j = turn(d + 1)
+            fwd_copy(j, 1 - t).wait_recv()
+            x = x_v[j].reshape(rows, width).astype(jnp.float32)
+            product = jnp.dot(
+                (x * gain).astype(jnp.bfloat16), wq_v[...], preferred_element_type=jnp.float32
+            )
+
+            @pl.when(j == c)
+            def _():
+                own_sum[...] = product
+
+            @pl.when(j != c)
+            def _():
+                part_out[j] = product.astype(jnp.bfloat16)
+                part_copy(j, c).start()
+
+        for d in range(1, n):
+            j = turn(d)
+            part_copy(j, j).wait_recv()
+            own_sum[...] += part_in[j].astype(jnp.float32)
+        remote(rs_out, rs_in, rs_send.at[0], rs_recv.at[0], s, c, 1 - t).wait_recv()
+        bias = b_qkv[pl.ds(layer, 1), :]
+        merged = (own_sum[...] * rs_in[:, :1] + bias).astype(jnp.bfloat16)
+        merged_v[...] = merged[:, :query_cols]
+        kv_v[c] = merged[:, query_cols:]
+        for k in range(n):
+            @pl.when(k > c)
+            def _():
+                kv_copy(k, c).start()
+                kv_v[k] = jnp.zeros((rows, 2 * HD), jnp.bfloat16)
+
+        for k in range(n):
+            @pl.when(k < c)
+            def _():
+                kv_copy(k, k).wait_recv()
+
+        query_pos = c * rows + lax.broadcasted_iota(jnp.int32, (rows, n * rows), 0)
+        allowed = lax.broadcasted_iota(jnp.int32, (rows, n * rows), 1) <= query_pos
+        keys = kv_v[:, :, :HD].reshape(n * rows, HD)
+        values = kv_v[:, :, HD:].reshape(n * rows, HD)
+        for h in range(GROUP):
+            q = merged_v[:, h * HD : (h + 1) * HD]
+            scores = lax.dot_general(
+                q, keys, (((1,), (1,)), ((), ())), preferred_element_type=jnp.float32
+            ) * HD ** (-0.5)
+            scores = jnp.where(allowed, scores, -1e30)
+            weights = jnp.exp(scores - jnp.max(scores, axis=1, keepdims=True))
+            total = jnp.sum(weights, axis=1, keepdims=True)
+            mixed = jnp.dot(
+                weights.astype(jnp.bfloat16), values, preferred_element_type=jnp.float32
+            ) / total
+            att_v[c, :, :, h * HD : (h + 1) * HD] = mixed.astype(jnp.bfloat16).reshape(2, half, HD)
+        for d in range(1, n):
+            att_copy(turn(d), c).start()
+        loads["wo"].wait()
+
+        @pl.loop(0, n)
+        def _(d):
+            j = turn(d)
+
+            @pl.when(d > 0)
+            def _():
+                att_copy(j, j).wait_recv()
+
+            half_out[j] = jnp.dot(
+                att_v[j, 1 - t], wo_v[...], preferred_element_type=jnp.float32
+            ).astype(jnp.bfloat16)
+            half_copy(j).start()
+            half_own[j] = x_v[j, t].astype(jnp.float32) + jnp.dot(
+                att_v[j, t], wo_v[...], preferred_element_type=jnp.float32
+            )
+
+        @pl.loop(0, n)
+        def _(d):
+            j = turn(d)
+            half_copy(j).wait_recv()
+            total = (half_own[j] + half_in[j].astype(jnp.float32)).astype(jnp.bfloat16)
+
+            @pl.when(d == 0)
+            def _():
+                res_v[c, t] = total
+                pair_copy(c, t).start()
+                out_copy(c, t).start()
+
+            @pl.when(d > 0)
+            def _():
+                half_out[n + j] = total
+                res_copy(j, c).start()
+
+        @pl.loop(1, n)
+        def _(d):
+            k = turn(d)
+            res_copy(k, k).wait_recv()
+            pair_copy(k, t).start()
+            out_copy(k, t).start()
+
+    @pl.loop(0, n)
+    def _(d):
+        k = turn(d)
+        pair_copy(k, 1 - t).wait_recv()
+        out_copy(k, 1 - t).start()
+
+    @pl.when(feeds)
+    def _():
+        for k in range(n):
+            x_copy(k).wait_send()
+        rs_copy().wait_send()
+
+    @pl.when(is_layer)
+    def _():
+        @pl.loop(0, n)
+        def _(d):
+            j = turn(d)
+            fwd_copy(j, t).wait_send()
+
+            @pl.when(d > 0)
+            def _():
+                part_copy(j, c).wait_send()
+                att_copy(j, c).wait_send()
+                res_copy(j, c).wait_send()
+
+            @pl.when(j > c)
+            def _():
+                kv_copy(j, c).wait_send()
+
+    @pl.loop(0, n)
+    def _(k):
+        half_copy(k).wait_send()
+        pair_copy(k, t).wait_send()
+        out_copy(k, 0).wait()
+        out_copy(k, 1).wait()
+
+
+def relayed(sizes, held, text, frames, join, ln_gain, w_proj, b_proj, norm_gain, w_qkv, b_qkv, w_out):
+    segs, n, rows, width = sizes
+    half = rows // 2
+    depth, qkv = w_qkv.shape[1:]
+    bf16, f32 = jnp.bfloat16, jnp.float32
+    hbm = pl.BlockSpec(memory_space=pl.ANY)
+    vmem = pl.BlockSpec(memory_space=pltpu.VMEM)
+    smem = pl.BlockSpec(memory_space=pltpu.SMEM)
+    dma = pltpu.SemaphoreType.DMA
+    out = pl.pallas_call(
+        partial(relay_kernel, sizes),
+        out_shape=jax.ShapeDtypeStruct((rows, n * width), bf16),
+        in_specs=[hbm, hbm, vmem, smem, vmem, hbm, vmem, vmem, hbm, vmem, hbm],
+        out_specs=hbm,
+        scratch_shapes=[
+            pltpu.VMEM((rows, n * width), bf16),
+            pltpu.VMEM((rows, HD), f32),
+            pltpu.VMEM((rows, HD), f32),
+            pltpu.VMEM((n, 2, half, width), bf16),
+            pltpu.VMEM((depth, qkv), bf16),
+            pltpu.VMEM(w_out.shape[1:], bf16),
+            pltpu.VMEM((rows, qkv), f32),
+            pltpu.VMEM((n, rows, qkv), bf16),
+            pltpu.VMEM((n, rows, qkv), bf16),
+            pltpu.VMEM((rows, GROUP * HD), bf16),
+            pltpu.VMEM((n, rows, 2 * HD), bf16),
+            pltpu.VMEM((n, 2, half, GROUP * HD), bf16),
+            pltpu.VMEM((2, half, w_proj.shape[0]), bf16),
+            pltpu.VMEM(w_proj.shape, bf16),
+            pltpu.VMEM((rows, n * width), bf16),
+            pltpu.VMEM((2 * n, half, width), bf16),
+            pltpu.VMEM((n, half, width), bf16),
+            pltpu.VMEM((n, half, width), f32),
+            pltpu.VMEM((n, 2, half, width), bf16),
+            dma((5,)), dma((n, 2)), dma((n,)), dma((n,)), dma((1,)), dma((1,)), dma((n,)), dma((n,)),
+            dma((n,)), dma((n,)), dma((n,)), dma((n,)), dma((n,)), dma((n,)),
+            dma((n,)), dma((n,)), dma((n,)), dma((n,)), dma((n,)), dma((n,)),
+        ],
+        compiler_params=pltpu.CompilerParams(
+            collective_id=0, has_side_effects=True, vmem_limit_bytes=56 * 1024 * 1024
+        ),
+    )(
+        held[0], text, frames, join, ln_gain[None], w_proj, b_proj[None], norm_gain, w_qkv, b_qkv, w_out
+    )
+    return out[None]
+
+
+def section(held, text, frames, join, ln_gain, w_proj, b_proj, norm_gain, w_qkv, b_qkv, w_out):
+    segs, n = lax.axis_size("segment"), lax.axis_size("ctx")
+    rows, width = held.shape[1], held.shape[2] // n
+    args = (held, text, frames, join, ln_gain, w_proj, b_proj, norm_gain, w_qkv, b_qkv, w_out)
+    whole_tiles = width % 128 == 0 and rows % 32 == 0 and w_proj.shape[0] % 128 == 0
+    if whole_tiles and n * rows <= 1024 and lax.axis_size("tp") == 2:
+        return relayed((segs, n, rows, width), *args)
+    return on_device(*args)
+
+
 def solution(mesh):
     return jax.shard_map(
-        on_device,
+        section,
         mesh=mesh,
         in_specs=(
             P("segment", "ctx", None),

time: 364 us -> 181 us (0.50)
  the two profiles are of different devices: /device:TPU:1 before, /device:TPU:4 now
where the time goes in v1:
time: 181 us; the launch traced here: 180 us
  Pallas kernels  176 us (97%)
  local copies, waits for them, and re-layouts  4.17 us (2%)
    pallas_call x1, Pallas kernels, relayed(): pl.pallas_call(partial(relay_kernel, sizes), out_shape=jax.ShapeDtypeStru...  176 us

profile of v1, /device:TPU:4, one launch (start us, length us, event | category | flops | bytes accessed | tf_op | source)
XLA Modules:
  0.0 180.5 jit_solution(2097029603343647412)
XLA Ops:
  0.0 1.3 broadcast_in_dim.10.b_proj
  1.3 176.3 %shard_map.109 = bf16[256,3584]{1,0:T(8,128)(2,1)} custom-call(bf16[256,3584]{1,0:T(8,128)(2,1)} %bitcast.4, bf16[256,3584]{1,0:T(8,128)(2,1)} %text.1, bf16[128,1024]{1,0:T(8,128)(2,1)} %frames.1, s32[2]{0:T(128)} %join.1, f32[1,1024]{1,0:T(1,128)} %bitcast.5, bf16[512,3584]{1,0:T(8,128)(2,1)} %w_proj.1, f32[1,3584]{1,0:T(1,128)} %broadcast_in_dim.10.b_proj, ...), custom_call_target="tpu_custom_call" | custom-call | tf_op jit(solution)/shard_map/pallas_call | solution.py:493
  177.6 2.8 %copy.13 = bf16[1,256,3584]{2,1,0:T(8,128)(2,1)} copy(bf16[1,256,3584]{2,1,0:T(8,128)(2,1)} %bitcast.3) | data formatting | bytes 3670016

commit v2 on v0

--- a/solution.py
+++ b/solution.py
@@ -3,6 +3,8 @@
 import jax
 import jax.numpy as jnp
 from jax import lax
+from jax.experimental import pallas as pl
+from jax.experimental.pallas import tpu as pltpu
 from jax.sharding import PartitionSpec as P
 
 HD = 128
@@ -139,9 +141,540 @@
     return result[None]
 
 
+def relay_kernel(
+    sizes,
+    held, text, frames, join, ln_gain, w_proj, b_proj, norm_gain, w_qkv, b_qkv, w_out,
+    out,
+    held_v, rs_out, rs_in, x_v, wq_v, wo_v, own_part, part_out, part_in, q_v, kv_v, att_v,
+    vis_v, wp_v, text_v, half_out, half_in, half_own, res_out, res_v, both, vis_out, vis_in, vis_own,
+    load_sem, store_sem, x_send, x_recv, rs_send, rs_recv, fwd_send, fwd_recv,
+    part_send, part_recv, kv_send, kv_recv, att_send, att_recv,
+    half_send, half_recv, res_send, res_recv, pair_send, pair_recv, vis_send, vis_recv,
+):
+    segs, n, rows, width = sizes
+    unit = rows // 2
+    half = unit // 2
+    last = segs - 1
+    s = lax.axis_index("segment")
+    c = lax.axis_index("ctx")
+    t = lax.axis_index("tp")
+    owner = jnp.where(s == 0, last, s)
+    layer = owner - 1
+    runs = (s < last, s > 0)
+    feeds = s < last
+    query_cols = GROUP * HD
+
+    def remote(src, dst, send, recv, segment, ctx, tp):
+        return pltpu.make_async_remote_copy(
+            src_ref=src, dst_ref=dst, send_sem=send, recv_sem=recv,
+            device_id={"segment": segment, "ctx": ctx, "tp": tp},
+            device_id_type=pl.DeviceIdType.MESH,
+        )
+
+    def cols(k):
+        return pl.ds(pl.multiple_of(k * width, 128), width)
+
+    def strip(r, side):
+        return pl.ds(pl.multiple_of(r * unit + side * half, 16), half)
+
+    def turn(d):
+        return lax.rem(c + d, n)
+
+    def far_first(i):
+        return jnp.where(2 * c < n, n - 1 - i, i)
+
+    loads = {
+        "held": pltpu.make_async_copy(held, held_v, load_sem.at[0]),
+        "wq": pltpu.make_async_copy(w_qkv.at[layer], wq_v, load_sem.at[1]),
+        "wo": pltpu.make_async_copy(w_out.at[layer], wo_v, load_sem.at[2]),
+        "wp": pltpu.make_async_copy(w_proj, wp_v, load_sem.at[3]),
+        "text": pltpu.make_async_copy(text, text_v, load_sem.at[4]),
+    }
+    barrier = pltpu.get_barrier_semaphore()
+
+    def greet(segment, ctx, tp):
+        pl.semaphore_signal(
+            barrier, inc=1, device_id={"segment": segment, "ctx": ctx, "tp": tp},
+            device_id_type=pl.DeviceIdType.MESH,
+        )
+
+    greet(s, c, 1 - t)
+    for d in range(1, n):
+        greet(s, turn(d), t)
+    for e in range(1, segs):
+        for d in range(n):
+            greet(lax.rem(s + e, segs), turn(d), t)
+
+    @pl.when(feeds)
+    def _():
+        loads["held"].start()
+
+    loads["wq"].start()
+    loads["wo"].start()
+
+    @pl.when(s == 0)
+    def _():
+        loads["wp"].start()
+        loads["text"].start()
+
+    for k in range(n):
+        @pl.when(k > c)
+        def _():
+            kv_v[k] = jnp.zeros((2, unit, 2 * HD), jnp.bfloat16)
+
+    kv_v[c, 1] = jnp.zeros((unit, 2 * HD), jnp.bfloat16)
+
+    pl.semaphore_wait(barrier, segs * n)
+
+    def x_copy(r, k):
+        worker = jnp.where(s == last - 1, 0, s + 1) if r == 0 else jnp.minimum(s + 1, last)
+        return remote(
+            held.at[strip(r, t), cols(k)], x_v.at[c, r, t],
+            x_send.at[r, k], x_recv.at[r, c], worker, k, t,
+        )
+
+    def rs_copy(to, slot):
+        return remote(rs_out, rs_in, rs_send.at[slot], rs_recv.at[0], to, c, t)
+
+    def fwd_copy(r, j, side):
+        return remote(
+            x_v.at[j, r, side], x_v.at[j, r, side], fwd_send.at[r, j], fwd_recv.at[r, j],
+            s, c, 1 - t,
+        )
+
+    def part_copy(r, k, to, slot):
+        return remote(
+            part_out.at[r, k], part_in.at[r, slot], part_send.at[r, k], part_recv.at[r, slot],
+            s, to, t,
+        )
+
+    def part_wait(r, slot):
+        part_copy(r, c, turn(1), slot).wait_recv()
+
+    def send_part(r, k):
+        @pl.when(k > c)
+        def _():
+            part_copy(r, k, jnp.minimum(c + 1, n - 1), k).start()
+
+        @pl.when(k < c)
+        def _():
+            to = jnp.maximum(c - 1, 0)
+            part_copy(r, k, to, jnp.where(k == to, n, k)).start()
+
+    def kv_copy(r, to, k, slot, side):
+        return remote(
+            kv_v.at[slot, r], kv_v.at[slot, r], kv_send.at[r, side, k], kv_recv.at[r, slot],
+            to, k, t,
+        )
+
+    def att_copy(r, k, slot):
+        return remote(
+            att_v.at[slot, r], att_v.at[slot, r], att_send.at[r, k], att_recv.at[r, slot], s, k, t
+        )
+
+    def half_copy(r, j):
+        return remote(
+            half_out.at[r, j], half_in.at[r, j], half_send.at[r, j], half_recv.at[r, j],
+            s, c, 1 - t,
+        )
+
+    def vis_copy(k):
+        return remote(vis_out.at[k], vis_in.at[k], vis_send.at[k], vis_recv.at[k], s, c, 1 - t)
+
+    def res_copy(r, j, slot):
+        return remote(
+            res_out.at[r, j], res_v.at[slot, r, t], res_send.at[r, j], res_recv.at[r, slot],
+            owner, j, t,
+        )
+
+    def pair_copy(r, k, side):
+        return remote(
+            res_v.at[k, r, side], res_v.at[k, r, side], pair_send.at[r, k], pair_recv.at[r, k],
+            s, c, 1 - t,
+        )
+
+    def out_copy(r, k, side):
+        return pltpu.make_async_copy(
+            res_v.at[k, r, side], out.at[strip(r, side), cols(k)], store_sem.at[r, k, side]
+        )
+
+    @pl.when(feeds)
+    def _():
+        for r in range(2):
+            for d in range(n):
+                x_copy(r, turn(d)).start()
+        loads["held"].wait()
+
+        @pl.loop(0, rows // 32)
+        def _(i):
+            at = pl.ds(pl.multiple_of(i * 32, 32), 32)
+            x = held_v[at, :].astype(jnp.float32)
+            scale = lax.rsqrt(jnp.mean(x * x, axis=1, keepdims=True) + 1e-06)
+            rs_out[at, :] = jnp.broadcast_to(scale, (32, HD))
+
+        rs_copy(s + 1, 0).start()
+
+        @pl.when(s == last - 1)
+        def _():
+            rs_copy(0, 1).start()
+
+    loads["wq"].wait()
+    gain = norm_gain[pl.ds(layer, 1), cols(c)]
+    bias = b_qkv[pl.ds(layer, 1), :]
+
+    for r in range(2):
+        @pl.when(runs[r])
+        def _():
+            @pl.loop(0, n)
+            def _(d):
+                j = turn(d)
+                remote(
+                    x_v.at[j, r, t], x_v.at[j, r, t], x_send.at[r, j], x_recv.at[r, j],
+                    s, c, 1 - t,
+                ).wait_recv()
+                fwd_copy(r, j, t).start()
+
+    for r in range(2):
+        @pl.when(runs[r])
+        def _():
+            @pl.loop(0, n)
+            def _(i):
+                j = far_first(i)
+                fwd_copy(r, j, 1 - t).wait_recv()
+                x = x_v[j, r].reshape(unit, width).astype(jnp.float32)
+                product = jnp.dot(
+                    (x * gain).astype(jnp.bfloat16), wq_v[...], preferred_element_type=jnp.float32
+                )
+                own_part[r, j] = product
+
+                @pl.when(((c == 0) | (c == n - 1)) & (j != c))
+                def _():
+                    part_out[r, j] = product.astype(jnp.bfloat16)
+                    send_part(r, j)
+
+    @pl.when(s == 0)
+    def _():
+        frame_in = frames[...].astype(jnp.float32)
+        center = jnp.mean(frame_in, axis=1, keepdims=True)
+        spread = jnp.mean((frame_in - center) * (frame_in - center), axis=1, keepdims=True)
+        normed = ((frame_in - center) * lax.rsqrt(spread + 1e-06) * ln_gain[...]).astype(
+            jnp.bfloat16
+        )
+        vis_width = w_proj.shape[0]
+        normed = jnp.where(t == 0, normed[:, :vis_width], normed[:, vis_width:])
+        count = frames.shape[0]
+        token = lax.broadcasted_iota(jnp.int32, (unit, count), 1)
+        row = lax.broadcasted_iota(jnp.int32, (unit, count), 0)
+        row = jnp.where(row < half, row, row + half)
+        for side in range(2):
+            position = c * rows + side * half + row
+            pick = jnp.zeros((unit, count), jnp.float32)
+            for f in range(count // FRAME):
+                mine = (token >= f * FRAME) & (token < (f + 1) * FRAME)
+                hit = mine & (position - join[f] == token - f * FRAME)
+                pick = jnp.where(hit, 1.0, pick)
+            vis_v[side] = jnp.dot(
+                pick.astype(jnp.bfloat16), normed, preferred_element_type=jnp.float32
+            ).astype(jnp.bfloat16)
+        loads["wp"].wait()
+        loads["text"].wait()
+
+        @pl.loop(0, n)
+        def _(k):
+            vis_out[k] = jnp.dot(
+                vis_v[1 - t], wp_v[:, cols(k)], preferred_element_type=jnp.float32
+            ).astype(jnp.bfloat16)
+            vis_copy(k).start()
+            vis_own[k] = jnp.dot(vis_v[t], wp_v[:, cols(k)], preferred_element_type=jnp.float32)
+
+    def pass_parts(r):
+        @pl.when(runs[r] & (c > 0) & (c < n - 1))
+        def _():
+            @pl.loop(0, n)
+            def _(i):
+                j = far_first(i)
+
+                @pl.when(j != c)
+                def _():
+                    part_wait(r, j)
+                    part_out[r, j] = (
+                        own_part[r, j] + part_in[r, j].astype(jnp.float32)
+                    ).astype(jnp.bfloat16)
+                    send_part(r, j)
+
+    def merge(r):
+        @pl.when(runs[r])
+        def _():
+            @pl.when(c > 0)
+            def _():
+                part_wait(r, c)
+                own_part[r, c] += part_in[r, c].astype(jnp.float32)
+
+            @pl.when(c < n - 1)
+            def _():
+                part_wait(r, n)
+                own_part[r, c] += part_in[r, n].astype(jnp.float32)
+
+            scale = rs_in[r * unit : (r + 1) * unit, :1]
+            merged = (own_part[r, c] * scale + bias).astype(jnp.bfloat16)
+            q_v[r] = merged[:, :query_cols]
+            kv_v[c, r] = merged[:, query_cols:]
+            for k in range(n):
+                @pl.when(k > c)
+                def _():
+                    kv_copy(r, s, k, c, 0).start()
+
+                @pl.when((k > c) & (owner == last))
+                def _():
+                    kv_copy(r, last - s, k, c, 1).start()
+
+            if r == 0:
+                @pl.when(s == 0)
+                def _():
+                    kv_copy(0, last, c, c, 1).start()
+
+    def attend(r):
+        @pl.when(runs[r])
+        def _():
+            take = (s < last) if r == 0 else (s == last)
+            for k in range(n):
+                @pl.when((k < c) & take)
+                def _():
+                    for part in range(2):
+                        kv_copy(part, s, turn(1), k, 0).wait_recv()
+
+            if r == 1:
+                @pl.when(s == last)
+                def _():
+                    kv_copy(0, s, turn(1), c, 0).wait_recv()
+
+            first = c * rows + r * unit
+            query_pos = first + lax.broadcasted_iota(jnp.int32, (unit, n * rows), 0)
+            allowed = lax.broadcasted_iota(jnp.int32, (unit, n * rows), 1) <= query_pos
+            keys = kv_v[:, :, :, :HD].reshape(n * rows, HD)
+            values = kv_v[:, :, :, HD:].reshape(n * rows, HD)
+            for h in range(GROUP):
+                q = q_v[r, :, h * HD : (h + 1) * HD]
+                scores = lax.dot_general(
+                    q, keys, (((1,), (1,)), ((), ())), preferred_element_type=jnp.float32
+                ) * HD ** (-0.5)
+                scores = jnp.where(allowed, scores, -1e30)
+                weights = jnp.exp(scores - jnp.max(scores, axis=1, keepdims=True))
+                total = jnp.sum(weights, axis=1, keepdims=True)
+                mixed = jnp.dot(
+                    weights.astype(jnp.bfloat16), values, preferred_element_type=jnp.float32
+                ) / total
+                att_v[c, r, :, h * HD : (h + 1) * HD] = mixed.astype(jnp.bfloat16)
+            for d in range(1, n):
+                att_copy(r, turn(d), c).start()
+
+    pass_parts(0)
+    remote(rs_out, rs_in, rs_send.at[0], rs_recv.at[0], s, c, 1 - t).wait_recv()
+    merge(0)
+    pass_parts(1)
+    merge(1)
+    attend(0)
+    attend(1)
+
+    @pl.when(s == 0)
+    def _():
+        row = lax.broadcasted_iota(jnp.int32, (half, width), 0)
+
+        @pl.loop(0, n)
+        def _(k):
+            vis_copy(k).wait_recv()
+            total = vis_own[k] + vis_in[k].astype(jnp.float32) + b_proj[:, cols(k)]
+            for r in range(2):
+                place = c * rows + r * unit + t * half + row
+                inside = jnp.zeros((half, width), jnp.bool_)
+                for f in range(frames.shape[0] // FRAME):
+                    inside = inside | ((place >= join[f]) & (place < join[f] + FRAME))
+                base = text_v[strip(r, t), cols(k)].astype(jnp.float32)
+                res_v[k, r, t] = jnp.where(
+                    inside, total[r * half : (r + 1) * half], base
+                ).astype(jnp.bfloat16)
+                pair_copy(r, k, t).start()
+                out_copy(r, k, t).start()
+
+    loads["wo"].wait()
+    for r in range(2):
+        @pl.when(runs[r])
+        def _():
+            @pl.loop(0, n)
+            def _(d):
+                j = turn(d)
+
+                @pl.when(d > 0)
+                def _():
+                    att_copy(r, j, j).wait_recv()
+
+                both[...] = jnp.dot(
+                    att_v[j, r], wo_v[...], preferred_element_type=jnp.float32
+                ).reshape(2, half, width)
+                half_out[r, j] = both[1 - t].astype(jnp.bfloat16)
+                half_copy(r, j).start()
+                half_own[r, j] = x_v[j, r, t].astype(jnp.float32) + both[t]
+
+    for r in range(2):
+        @pl.when(runs[r])
+        def _():
+            @pl.loop(0, n)
+            def _(d):
+                j = turn(d)
+                half_copy(r, j).wait_recv()
+                total = (half_own[r, j] + half_in[r, j].astype(jnp.float32)).astype(jnp.bfloat16)
+
+                @pl.when((d == 0) & (s > 0))
+                def _():
+                    res_v[c, r, t] = total
+                    pair_copy(r, c, t).start()
+                    out_copy(r, c, t).start()
+
+                @pl.when((d > 0) | (s == 0))
+                def _():
+                    res_out[r, j] = total
+                    res_copy(r, j, c).start()
+
+    for r in range(2):
+        @pl.when(s > 0)
+        def _():
+            @pl.loop(0, n)
+            def _(d):
+                k = turn(d)
+
+                @pl.when((d > 0) | ((s == last) & (r == 0)))
+                def _():
+                    remote(
+                        res_out.at[r, k], res_v.at[k, r, t], res_send.at[r, k], res_recv.at[r, k],
+                        s, c, 1 - t,
+                    ).wait_recv()
+                    pair_copy(r, k, t).start()
+                    out_copy(r, k, t).start()
+
+    for r in range(2):
+        @pl.loop(0, n)
+        def _(d):
+            k = turn(d)
+            pair_copy(r, k, 1 - t).wait_recv()
+            out_copy(r, k, 1 - t).start()
+
+    @pl.when(feeds)
+    def _():
+        for r in range(2):
+            for k in range(n):
+                x_copy(r, k).wait_send()
+        rs_copy(s + 1, 0).wait_send()
+
+        @pl.when(s == last - 1)
+        def _():
+            rs_copy(0, 1).wait_send()
+
+    @pl.when(s == 0)
+    def _():
+        kv_copy(0, last, c, c, 1).wait_send()
+        for k in range(n):
+            vis_copy(k).wait_send()
+
+    for r in range(2):
+        @pl.when(runs[r])
+        def _():
+            @pl.loop(0, n)
+            def _(d):
+                j = turn(d)
+                fwd_copy(r, j, t).wait_send()
+                half_copy(r, j).wait_send()
+
+                @pl.when(d > 0)
+                def _():
+                    part_copy(r, j, turn(1), c).wait_send()
+                    att_copy(r, j, c).wait_send()
+
+                @pl.when((d > 0) | (s == 0))
+                def _():
+                    res_copy(r, j, c).wait_send()
+
+                @pl.when(j > c)
+                def _():
+                    kv_copy(r, s, j, c, 0).wait_send()
+
+                @pl.when((j > c) & (owner == last))
+                def _():
+                    kv_copy(r, last - s, j, c, 1).wait_send()
+
+        @pl.loop(0, n)
+        def _(k):
+            pair_copy(r, k, t).wait_send()
+            out_copy(r, k, 0).wait()
+            out_copy(r, k, 1).wait()
+
+
+def relayed(sizes, held, text, frames, join, ln_gain, w_proj, b_proj, norm_gain, w_qkv, b_qkv, w_out):
+    segs, n, rows, width = sizes
+    unit = rows // 2
+    half = unit // 2
+    depth, qkv = w_qkv.shape[1:]
+    bf16, f32 = jnp.bfloat16, jnp.float32
+    hbm = pl.BlockSpec(memory_space=pl.ANY)
+    vmem = pl.BlockSpec(memory_space=pltpu.VMEM)
+    smem = pl.BlockSpec(memory_space=pltpu.SMEM)
+    dma = pltpu.SemaphoreType.DMA
+    out = pl.pallas_call(
+        partial(relay_kernel, sizes),
+        out_shape=jax.ShapeDtypeStruct((rows, n * width), bf16),
+        in_specs=[hbm, hbm, vmem, smem, vmem, hbm, vmem, vmem, hbm, vmem, hbm],
+        out_specs=hbm,
+        scratch_shapes=[
+            pltpu.VMEM((rows, n * width), bf16),
+            pltpu.VMEM((rows, HD), f32),
+            pltpu.VMEM((rows, HD), f32),
+            pltpu.VMEM((n, 2, 2, half, width), bf16),
+            pltpu.VMEM((depth, qkv), bf16),
+            pltpu.VMEM(w_out.shape[1:], bf16),
+            pltpu.VMEM((2, n, unit, qkv), f32),
+            pltpu.VMEM((2, n, unit, qkv), bf16),
+            pltpu.VMEM((2, n + 1, unit, qkv), bf16),
+            pltpu.VMEM((2, unit, GROUP * HD), bf16),
+            pltpu.VMEM((n, 2, unit, 2 * HD), bf16),
+            pltpu.VMEM((n, 2, unit, GROUP * HD), bf16),
+            pltpu.VMEM((2, unit, w_proj.shape[0]), bf16),
+            pltpu.VMEM(w_proj.shape, bf16),
+            pltpu.VMEM((rows, n * width), bf16),
+            pltpu.VMEM((2, n, half, width), bf16),
+            pltpu.VMEM((2, n, half, width), bf16),
+            pltpu.VMEM((2, n, half, width), f32),
+            pltpu.VMEM((2, n, half, width), bf16),
+            pltpu.VMEM((n, 2, 2, half, width), bf16),
+            pltpu.VMEM((2, half, width), f32),
+            pltpu.VMEM((n, unit, width), bf16),
+            pltpu.VMEM((n, unit, width), bf16),
+            pltpu.VMEM((n, unit, width), f32),
+            dma((5,)), dma((2, n, 2)), dma((2, n)), dma((2, n)), dma((2,)), dma((1,)),
+            dma((2, n)), dma((2, n)), dma((2, n)), dma((2, n + 1)), dma((2, 2, n)), dma((2, n)),
+            dma((2, n)), dma((2, n)), dma((2, n)), dma((2, n)), dma((2, n)), dma((2, n)),
+            dma((2, n)), dma((2, n)), dma((n,)), dma((n,)),
+        ],
+        compiler_params=pltpu.CompilerParams(
+            collective_id=0, has_side_effects=True, vmem_limit_bytes=60 * 1024 * 1024
+        ),
+    )(
+        held[0], text, frames, join, ln_gain[None], w_proj, b_proj[None], norm_gain, w_qkv, b_qkv, w_out
+    )
+    return out[None]
+
+
+def section(held, text, frames, join, ln_gain, w_proj, b_proj, norm_gain, w_qkv, b_qkv, w_out):
+    segs, n = lax.axis_size("segment"), lax.axis_size("ctx")
+    rows, width = held.shape[1], held.shape[2] // n
+    args = (held, text, frames, join, ln_gain, w_proj, b_proj, norm_gain, w_qkv, b_qkv, w_out)
+    whole_tiles = width % 128 == 0 and rows % 64 == 0 and w_proj.shape[0] % 128 == 0
+    if whole_tiles and n * rows <= 1024 and lax.axis_size("tp") == 2 and segs > 2:
+        return relayed((segs, n, rows, width), *args)
+    return on_device(*args)
+
+
 def solution(mesh):
     return jax.shard_map(
-        on_device,
+        section,
         mesh=mesh,
         in_specs=(
             P("segment", "ctx", None),

time: 364 us -> 138 us (0.38)
  waiting for transfers between devices: 275 us -> 0 us
  Pallas kernels: 0 us -> 131 us
  blocking collectives: 33.2 us -> 0 us
  matrix products: 16.7 us -> 0 us
  between operations: 14.6 us -> 0.01 us
  other arithmetic: 9.7 us -> 0 us
  starting transfers between devices: 4.62 us -> 0 us
  local copies, waits for them, and re-layouts: 8.27 us -> 4.17 us
    all_gather x2 -> x0, waiting for transfers between devices: 197 us -> none  [the longest x1 122 us: on_device(): lax.all_gather(weight_qkv, 'ctx', axis=0, tiled=True)]
    pallas_call x0 -> x1, Pallas kernels: none -> 131 us  [relayed(): pl.pallas_call(partial(relay_kernel, sizes), out_shape=jax.ShapeDtypeStru...]
    psum x1 -> x0, waiting for transfers between devices: 61.9 us -> none  [on_device(): lax.psum(section_term.astype(jnp.bfloat16), 'tp').astype(jnp.float32)]
    all_gather x2 -> x0, blocking collectives: 33.2 us -> none  [the longest x1 20.3 us: on_device(): values_in = lax.all_gather(value_part, 'ctx', axis=0, tiled=True)]
    dot_general x6 -> x0, matrix products: 16.7 us -> none  [the longest x1 6.11 us: on_device(): jnp.dot(attended, lax.all_gather(weight_out, 'ctx', axis=1, tiled=True),...]
    ppermute x1 -> x0, waiting for transfers between devices: 16.6 us -> none  [shifted(): return lax.ppermute(value, axis, pairs)]
    dynamic_slice x4 -> x0, local copies, waits for them, and re-layouts: 6.59 us -> none  [the longest x1 3.08 us: on_device(): weight_qkv = lax.dynamic_index_in_dim(w_qkv, layer_id, 0, keepdims=False)]
    broadcast_in_dim x1 -> x0, other arithmetic: 4.81 us -> none  [on_device(): return result[None]]
  transfers between devices with their start and end apart: 4 -> 0, of which waited for: 4 -> 0; matrix products, arithmetic and copies ran while one was open for 6% -> 0% of each run, Pallas kernels for 0% -> 0%
where the time goes in v2:
time: 138 us; the launch traced here: 135 us
  Pallas kernels  131 us (95%)
  local copies, waits for them, and re-layouts  4.17 us (3%)
    pallas_call x1, Pallas kernels, relayed(): pl.pallas_call(partial(relay_kernel, sizes), out_shape=jax.ShapeDtypeStru...  131 us
    unnamed x1, local copies, waits for them, and re-layouts  2.85 us

profile of v2, /device:TPU:1, one launch (start us, length us, event | category | flops | bytes accessed | tf_op | source)
XLA Modules:
  0.0 135.4 jit_solution(3921129972542239655)
XLA Ops:
  0.0 1.3 broadcast_in_dim.10.b_proj
  1.3 131.2 %shard_map.109 = bf16[256,3584]{1,0:T(8,128)(2,1)} custom-call(bf16[256,3584]{1,0:T(8,128)(2,1)} %bitcast.4, bf16[256,3584]{1,0:T(8,128)(2,1)} %text.1, bf16[128,1024]{1,0:T(8,128)(2,1)} %frames.1, s32[2]{0:T(128)} %join.1, f32[1,1024]{1,0:T(1,128)} %bitcast.5, bf16[512,3584]{1,0:T(8,128)(2,1)} %w_proj.1, f32[1,3584]{1,0:T(1,128)} %broadcast_in_dim.10.b_proj, ...), custom_call_target="tpu_custom_call" | custom-call | tf_op jit(solution)/shard_map/pallas_call | solution.py:621
  132.5 2.8 %copy.13 = bf16[1,256,3584]{2,1,0:T(8,128)(2,1)} copy(bf16[1,256,3584]{2,1,0:T(8,128)(2,1)} %bitcast.3) | data formatting | bytes 3670016

commit v3 on v2

--- a/solution.py
+++ b/solution.py
@@ -183,6 +183,9 @@
     def far_first(i):
         return jnp.where(2 * c < n, n - 1 - i, i)
 
+    def near_first(i):
+        return jnp.where(2 * c < n, i, n - 1 - i)
+
     loads = {
         "held": pltpu.make_async_copy(held, held_v, load_sem.at[0]),
         "wq": pltpu.make_async_copy(w_qkv.at[layer], wq_v, load_sem.at[1]),
@@ -267,10 +270,26 @@
             to, k, t,
         )
 
-    def att_copy(r, k, slot):
+    def att_copy(r, to, slot, sem):
         return remote(
-            att_v.at[slot, r], att_v.at[slot, r], att_send.at[r, k], att_recv.at[r, slot], s, k, t
-        )
+            att_v.at[slot, r], att_v.at[slot, r], att_send.at[r, sem], att_recv.at[r, slot],
+            s, to, t,
+        )
+
+    up, down = jnp.minimum(c + 1, n - 1), jnp.maximum(c - 1, 0)
+
+    def each_hop(r, j, act):
+        @pl.when((j <= c) & (c < n - 1))
+        def _():
+            act(att_copy(r, up, j, j))
+
+        @pl.when((j == c) & (c > 0))
+        def _():
+            act(att_copy(r, down, j, n))
+
+        @pl.when((j > c) & (c > 0))
+        def _():
+            act(att_copy(r, down, j, j))
 
     def half_copy(r, j):
         return remote(
@@ -322,35 +341,50 @@
     gain = norm_gain[pl.ds(layer, 1), cols(c)]
     bias = b_qkv[pl.ds(layer, 1), :]
 
-    for r in range(2):
+    def hand_over(r, i):
         @pl.when(runs[r])
         def _():
-            @pl.loop(0, n)
-            def _(d):
-                j = turn(d)
-                remote(
-                    x_v.at[j, r, t], x_v.at[j, r, t], x_send.at[r, j], x_recv.at[r, j],
-                    s, c, 1 - t,
-                ).wait_recv()
-                fwd_copy(r, j, t).start()
-
-    for r in range(2):
+            j = turn(i)
+            remote(
+                x_v.at[j, r, t], x_v.at[j, r, t], x_send.at[r, j], x_recv.at[r, j], s, c, 1 - t
+            ).wait_recv()
+            fwd_copy(r, j, t).start()
+
+    def multiply(r, i):
         @pl.when(runs[r])
         def _():
-            @pl.loop(0, n)
-            def _(i):
-                j = far_first(i)
-                fwd_copy(r, j, 1 - t).wait_recv()
-                x = x_v[j, r].reshape(unit, width).astype(jnp.float32)
-                product = jnp.dot(
-                    (x * gain).astype(jnp.bfloat16), wq_v[...], preferred_element_type=jnp.float32
-                )
-                own_part[r, j] = product
-
-                @pl.when(((c == 0) | (c == n - 1)) & (j != c))
-                def _():
-                    part_out[r, j] = product.astype(jnp.bfloat16)
-                    send_part(r, j)
+            j = far_first(i)
+            fwd_copy(r, j, 1 - t).wait_recv()
+            x = x_v[j, r].reshape(unit, width).astype(jnp.float32)
+            product = jnp.dot(
+                (x * gain).astype(jnp.bfloat16), wq_v[...], preferred_element_type=jnp.float32
+            )
+            own_part[r, j] = product
+
+            @pl.when(((c == 0) | (c == n - 1)) & (j != c))
+            def _():
+                part_out[r, j] = product.astype(jnp.bfloat16)
+                send_part(r, j)
+
+    def pass_part(r, i):
+        j = far_first(i)
+
+        @pl.when(runs[r] & (c > 0) & (c < n - 1) & (j != c))
+        def _():
+            part_wait(r, j)
+            part_out[r, j] = (
+                own_part[r, j] + part_in[r, j].astype(jnp.float32)
+            ).astype(jnp.bfloat16)
+            send_part(r, j)
+
+    @pl.loop(0, n)
+    def _(i):
+        hand_over(0, i)
+
+    @pl.loop(0, n)
+    def _(i):
+        multiply(0, i)
+        hand_over(1, i)
 
     @pl.when(s == 0)
     def _():
@@ -387,20 +421,10 @@
             vis_copy(k).start()
             vis_own[k] = jnp.dot(vis_v[t], wp_v[:, cols(k)], preferred_element_type=jnp.float32)
 
-    def pass_parts(r):
-        @pl.when(runs[r] & (c > 0) & (c < n - 1))
-        def _():
-            @pl.loop(0, n)
-            def _(i):
-                j = far_first(i)
-
-                @pl.when(j != c)
-                def _():
-                    part_wait(r, j)
-                    part_out[r, j] = (
-                        own_part[r, j] + part_in[r, j].astype(jnp.float32)
-                    ).astype(jnp.bfloat16)
-                    send_part(r, j)
+    @pl.loop(0, n)
+    def _(i):
+        multiply(1, i)
+        pass_part(0, i)
 
     def merge(r):
         @pl.when(runs[r])
@@ -465,13 +489,15 @@
                     weights.astype(jnp.bfloat16), values, preferred_element_type=jnp.float32
                 ) / total
                 att_v[c, r, :, h * HD : (h + 1) * HD] = mixed.astype(jnp.bfloat16)
-            for d in range(1, n):
-                att_copy(r, turn(d), c).start()
-
-    pass_parts(0)
+            each_hop(r, c, lambda copy: copy.start())
+
     remote(rs_out, rs_in, rs_send.at[0], rs_recv.at[0], s, c, 1 - t).wait_recv()
     merge(0)
-    pass_parts(1)
+
+    @pl.loop(0, n)
+    def _(i):
+        pass_part(1, i)
+
     merge(1)
     attend(0)
     attend(1)
@@ -496,60 +522,72 @@
                 pair_copy(r, k, t).start()
                 out_copy(r, k, t).start()
 
+    def project(r, i):
+        @pl.when(runs[r])
+        def _():
+            j = near_first(i)
+
+            @pl.when(j != c)
+            def _():
+                att_copy(r, turn(1), j, j).wait_recv()
+                each_hop(r, j, lambda copy: copy.start())
+
+            both[...] = jnp.dot(
+                att_v[j, r], wo_v[...], preferred_element_type=jnp.float32
+            ).reshape(2, half, width)
+            half_out[r, j] = both[1 - t].astype(jnp.bfloat16)
+            half_copy(r, j).start()
+            half_own[r, j] = x_v[j, r, t].astype(jnp.float32) + both[t]
+
+    def deliver(r, i):
+        @pl.when(runs[r])
+        def _():
+            j = near_first(i)
+            half_copy(r, j).wait_recv()
+            total = (half_own[r, j] + half_in[r, j].astype(jnp.float32)).astype(jnp.bfloat16)
+
+            @pl.when((j == c) & (s > 0))
+            def _():
+                res_v[c, r, t] = total
+                pair_copy(r, c, t).start()
+                out_copy(r, c, t).start()
+
+            @pl.when((j != c) | (s == 0))
+            def _():
+                res_out[r, j] = total
+                res_copy(r, j, c).start()
+
+    def collect(r, i):
+        k = near_first(i)
+
+        @pl.when((s > 0) & ((k != c) | ((s == last) & (r == 0))))
+        def _():
+            remote(
+                res_out.at[r, k], res_v.at[k, r, t], res_send.at[r, k], res_recv.at[r, k],
+                s, c, 1 - t,
+            ).wait_recv()
+            pair_copy(r, k, t).start()
+            out_copy(r, k, t).start()
+
     loads["wo"].wait()
-    for r in range(2):
-        @pl.when(runs[r])
-        def _():
-            @pl.loop(0, n)
-            def _(d):
-                j = turn(d)
-
-                @pl.when(d > 0)
-                def _():
-                    att_copy(r, j, j).wait_recv()
-
-                both[...] = jnp.dot(
-                    att_v[j, r], wo_v[...], preferred_element_type=jnp.float32
-                ).reshape(2, half, width)
-                half_out[r, j] = both[1 - t].astype(jnp.bfloat16)
-                half_copy(r, j).start()
-                half_own[r, j] = x_v[j, r, t].astype(jnp.float32) + both[t]
-
-    for r in range(2):
-        @pl.when(runs[r])
-        def _():
-            @pl.loop(0, n)
-            def _(d):
-                j = turn(d)
-                half_copy(r, j).wait_recv()
-                total = (half_own[r, j] + half_in[r, j].astype(jnp.float32)).astype(jnp.bfloat16)
-
-                @pl.when((d == 0) & (s > 0))
-                def _():
-                    res_v[c, r, t] = total
-                    pair_copy(r, c, t).start()
-                    out_copy(r, c, t).start()
-
-                @pl.when((d > 0) | (s == 0))
-                def _():
-                    res_out[r, j] = total
-                    res_copy(r, j, c).start()
-
-    for r in range(2):
-        @pl.when(s > 0)
-        def _():
-            @pl.loop(0, n)
-            def _(d):
-                k = turn(d)
-
-                @pl.when((d > 0) | ((s == last) & (r == 0)))
-                def _():
-                    remote(
-                        res_out.at[r, k], res_v.at[k, r, t], res_send.at[r, k], res_recv.at[r, k],
-                        s, c, 1 - t,
-                    ).wait_recv()
-                    pair_copy(r, k, t).start()
-                    out_copy(r, k, t).start()
+
+    @pl.loop(0, n)
+    def _(i):
+        project(0, i)
+
+    @pl.loop(0, n)
+    def _(i):
+        deliver(0, i)
+        project(1, i)
+
+    @pl.loop(0, n)
+    def _(i):
+        deliver(1, i)
+        collect(0, i)
+
+    @pl.loop(0, n)
+    def _(i):
+        collect(1, i)
 
     for r in range(2):
         @pl.loop(0, n)
@@ -587,7 +625,8 @@
                 @pl.when(d > 0)
                 def _():
                     part_copy(r, j, turn(1), c).wait_send()
-                    att_copy(r, j, c).wait_send()
+
+                each_hop(r, j, lambda copy: copy.wait_send())
 
                 @pl.when((d > 0) | (s == 0))
                 def _():
@@ -650,7 +689,7 @@
             pltpu.VMEM((n, unit, width), f32),
             dma((5,)), dma((2, n, 2)), dma((2, n)), dma((2, n)), dma((2,)), dma((1,)),
             dma((2, n)), dma((2, n)), dma((2, n)), dma((2, n + 1)), dma((2, 2, n)), dma((2, n)),
-            dma((2, n)), dma((2, n)), dma((2, n)), dma((2, n)), dma((2, n)), dma((2, n)),
+            dma((2, n + 1)), dma((2, n)), dma((2, n)), dma((2, n)), dma((2, n)), dma((2, n)),
             dma((2, n)), dma((2, n)), dma((n,)), dma((n,)),
         ],
         compiler_params=pltpu.CompilerParams(

time: 138 us -> 124 us (0.90); the launches traced: 135 us -> 123 us
  Pallas kernels: 131 us -> 119 us
    pallas_call x1, Pallas kernels: 131 us -> 119 us  [relayed(): pl.pallas_call(partial(relay_kernel, sizes), out_shape=jax.ShapeDtypeStru...]
where the time goes in v3:
time: 124 us; the launch traced here: 123 us
  Pallas kernels  119 us (96%)
  local copies, waits for them, and re-layouts  4.17 us (3%)
    pallas_call x1, Pallas kernels, relayed(): pl.pallas_call(partial(relay_kernel, sizes), out_shape=jax.ShapeDtypeStru...  119 us
    unnamed x1, local copies, waits for them, and re-layouts  2.85 us

profile of v3, /device:TPU:1, one launch (start us, length us, event | category | flops | bytes accessed | tf_op | source)
XLA Modules:
  0.0 123.4 jit_solution(15710814984639322219)
XLA Ops:
  0.0 1.3 %broadcast_in_dim.10.b_proj = f32[1,3584]{1,0:T(1,128)} reshape(f32[3584]{0:T(1024)} %param.17) | data formatting | bytes 28672 | tf_op jit(solution)/shard_map/broadcast_in_dim | solution.py:699
  1.3 119.2 %shard_map.109 = bf16[256,3584]{1,0:T(8,128)(2,1)} custom-call(bf16[256,3584]{1,0:T(8,128)(2,1)} %bitcast.4, bf16[256,3584]{1,0:T(8,128)(2,1)} %text.1, bf16[128,1024]{1,0:T(8,128)(2,1)} %frames.1, s32[2]{0:T(128)} %join.1, f32[1,1024]{1,0:T(1,128)} %bitcast.5, bf16[512,3584]{1,0:T(8,128)(2,1)} %w_proj.1, f32[1,3584]{1,0:T(1,128)} %broadcast_in_dim.10.b_proj, ...), custom_call_target="tpu_custom_call" | custom-call | tf_op jit(solution)/shard_map/pallas_call | solution.py:660
  120.5 2.8 %copy.13 = bf16[1,256,3584]{2,1,0:T(8,128)(2,1)} copy(bf16[1,256,3584]{2,1,0:T(8,128)(2,1)} %bitcast.3) | data formatting | bytes 3670016

commit v4 on v3

--- a/solution.py
+++ b/solution.py
@@ -509,7 +509,7 @@
         @pl.loop(0, n)
         def _(k):
             vis_copy(k).wait_recv()
-            total = vis_own[k] + vis_in[k].astype(jnp.float32) + b_proj[:, cols(k)]
+            total = vis_own[k] + vis_in[k].astype(jnp.float32) + b_proj[cols(k)][None]
             for r in range(2):
                 place = c * rows + r * unit + t * half + row
                 inside = jnp.zeros((half, width), jnp.bool_)
@@ -696,7 +696,7 @@
             collective_id=0, has_side_effects=True, vmem_limit_bytes=60 * 1024 * 1024
         ),
     )(
-        held[0], text, frames, join, ln_gain[None], w_proj, b_proj[None], norm_gain, w_qkv, b_qkv, w_out
+        held[0], text, frames, join, ln_gain[None], w_proj, b_proj, norm_gain, w_qkv, b_qkv, w_out
     )
     return out[None]
 

time: 124 us -> 122 us (0.984)
  local copies, waits for them, and re-layouts: 4.17 us -> 2.85 us
    broadcast_in_dim x1 -> x0, local copies, waits for them, and re-layouts: 1.33 us -> none  [relayed(): b_proj[None]]
where the time goes in v4:
time: 122 us
  Pallas kernels  119 us (98%)
  local copies, waits for them, and re-layouts  2.85 us (2%)
    pallas_call x1, Pallas kernels, relayed(): pl.pallas_call(partial(relay_kernel, sizes), out_shape=jax.ShapeDtypeStru...  119 us
    unnamed x1, local copies, waits for them, and re-layouts  2.85 us

profile of v4, /device:TPU:1, one launch (start us, length us, event | category | flops | bytes accessed | tf_op | source)
XLA Modules:
  0.0 122.0 jit_solution(14133505100692731615)
XLA Ops:
  0.0 119.2 %shard_map.109 = bf16[256,3584]{1,0:T(8,128)(2,1)} custom-call(bf16[256,3584]{1,0:T(8,128)(2,1)} %bitcast.4, bf16[256,3584]{1,0:T(8,128)(2,1)} %text.1, bf16[128,1024]{1,0:T(8,128)(2,1)} %frames.1, s32[2]{0:T(128)} %join.1, f32[1,1024]{1,0:T(1,128)} %bitcast.5, bf16[512,3584]{1,0:T(8,128)(2,1)} %w_proj.1, f32[3584]{0:T(1024)} %b_proj.1, ...), custom_call_target="tpu_custom_call" | custom-call | tf_op jit(solution)/shard_map/pallas_call | solution.py:660
  119.2 2.8 %copy.13 = bf16[1,256,3584]{2,1,0:T(8,128)(2,1)} copy(bf16[1,256,3584]{2,1,0:T(8,128)(2,1)} %bitcast.3) | data formatting | bytes 3670016
